TPU v7x, 32 devices: a whole 2x2x4 slice. The times are simulated.
32 devices in a mesh: grp: 2 (over x), bus: 16 (over z, y, core).
Axes of the slice: x: 2, y: 2, z: 4, core: 2. Of those that a mesh axis runs over, the one named last changes fastest.
Arguments:
- loads: float32 [16384, 128], P(('grp', 'bus')), parts along dimension 0, may hold values from -4 to 4
- bus_type: int32 [16384], P(('grp', 'bus')), parts along dimension 0, may hold values from 0 to 2
- bus_slot: int32 [16384], P(('grp', 'bus')), parts along dimension 0, may hold values from 0 to 511, as said below
- block_inverse: float32 [128, 2, 128, 128], P(('grp', 'bus')), parts along dimension 0, may hold values from -1.5 to 1.5
- schur_inverse: float32 [2, 2048, 1024], P(None, ('grp', 'bus')), parts along dimension 1, may hold values from -1.5 to 1.5
- branch_bus: int32 [8192], P(('grp', 'bus')), parts along dimension 0, may hold values from 0 to 511
- branch_iface: int32 [8192], P(('grp', 'bus')), parts along dimension 0, may hold values from 0 to 1023, as said below
- branch_adm: float32 [2, 8192], P(None, ('grp', 'bus')), parts along dimension 1, may hold values from -4 to 4
Outputs:
- voltage: float32 [16384, 128], P(('grp', 'bus')), parts along dimension 0
- last_term: float32 [16384, 128], P(('grp', 'bus')), parts along dimension 0
There are 2 independent parts, one for each index of `grp`. A program takes and returns all parts, laid end to end along the dimension named above; each array names one. Nothing has to cross between parts.
Inputs may be any that keep to these rules, and one draw needn't show every extreme that they name: Within each device's 4 * 128 buses, bus_slot is a permutation of 0 to 511. `branch_iface`: A branch of device d names an interface row from max(d - 1, 0) * 64 to min(d + 2, 16) * 64 - 1.
All inputs are finite; a program needn't handle non-finite values.
Results may differ from a plain program's by a relative error of at most 0.00027.
Values sent between devices are 32-bit elements; how exact they have to be, the bound alone decides.
A program may use at most 64 MiB of HBM per device.

v0:
```python
import jax
import jax.numpy as jnp
from jax import lax
from jax.sharding import PartitionSpec as P

ORDERS = 4


highest = lax.Precision.HIGHEST


def shifted(block, axis, distance):
    devices = range(lax.axis_size(axis))
    route = [(i - distance, i) for i in devices if i - distance in devices]
    return lax.ppermute(block, axis, route)


def padded(x, sides, width):
    for axis, dim in sides:
        peers, length = (lax.axis_size(axis), x.shape[dim])
        up = [(i, (i + 1) % peers) for i in range(peers - 1)]
        down = [(j, i) for i, j in up]
        last = lax.slice_in_dim(x, length - width, length, axis=dim)
        initial = lax.slice_in_dim(x, 0, width, axis=dim)
        before = lax.ppermute(last, axis, up)
        after = lax.ppermute(initial, axis, down)
        x = jnp.concatenate([before, x, after], axis=dim)
    return x


def complex_mul(first, second):
    width = first.shape[-1] // 2
    first_real, first_imag = (first[..., :width], first[..., width:])
    second_real, second_imag = (second[..., :width], second[..., width:])
    return jnp.concatenate(
        [
            first_real * second_real - first_imag * second_imag,
            first_real * second_imag + first_imag * second_real,
        ],
        axis=-1,
    )


def conjugate(values):
    width = values.shape[-1] // 2
    return jnp.concatenate([values[..., :width], -values[..., width:]], axis=-1)


def rotate(values):
    width = values.shape[-1] // 2
    return jnp.concatenate([-values[..., width:], values[..., :width]], axis=-1)


def admit(values, adm_real, adm_imag):
    return values * adm_real + rotate(values) * adm_imag


def block_solve(inverse, right_side):
    count, rows = (inverse.shape[0], inverse.shape[2])
    blocks = right_side.reshape(count, rows, right_side.shape[-1])
    real_term = jnp.einsum(
        "pij,pjc->pic", inverse[:, 0], blocks, precision=highest, preferred_element_type=jnp.float32
    )
    imag_term = jnp.einsum(
        "pij,pjc->pic", inverse[:, 1], blocks, precision=highest, preferred_element_type=jnp.float32
    )
    return (real_term + rotate(imag_term)).reshape(count * rows, right_side.shape[-1])


def local(
    loads, bus_type, bus_slot, block_inverse, schur_inverse, branch_bus, branch_iface, branch_adm
):
    bus_rows = loads.shape[0]
    columns = loads.shape[1]
    width = columns // 2
    if_rows = schur_inverse.shape[1]
    placing = jnp.argsort(bus_slot)
    placed_loads = loads[placing]
    placed_type = bus_type[placing]
    branch_pos = bus_slot[branch_bus]
    relative = branch_iface - (lax.axis_index("bus") - 1) * if_rows
    adm_real = branch_adm[0][:, None]
    adm_imag = branch_adm[1][:, None]
    spread = (jnp.arange(bus_rows, dtype=jnp.int32)[:, None] == branch_pos[None, :]).astype(
        jnp.float32
    )
    near_select = (jnp.arange(3 * if_rows, dtype=jnp.int32)[:, None] == relative[None, :]).astype(
        jnp.float32
    )
    unit = jnp.concatenate(
        [jnp.ones((bus_rows, width), jnp.float32), jnp.zeros((bus_rows, width), jnp.float32)],
        axis=-1,
    )
    load_mask = (placed_type == 0)[:, None]
    current_mask = (placed_type == 1)[:, None]
    coeffs = [unit]
    inverses = [unit]
    for degree in range(1, ORDERS + 1):
        driven = jnp.where(load_mask, conjugate(complex_mul(placed_loads, inverses[-1])), 0.0)
        if degree == 1:
            driven = driven + jnp.where(current_mask, conjugate(placed_loads), 0.0)
        local_solution = block_solve(block_inverse, driven)
        flows = admit(local_solution[branch_pos], adm_real, adm_imag)
        near_sums = jnp.dot(
            near_select, flows, precision=highest, preferred_element_type=jnp.float32
        )
        middle_rows = near_sums[if_rows : 2 * if_rows]
        lower_rows = near_sums[:if_rows]
        upper_rows = near_sums[2 * if_rows :]
        from_below = shifted(upper_rows, "bus", 1)
        from_above = shifted(lower_rows, "bus", -1)
        own_sums = middle_rows + from_below + from_above
        piece = lax.all_gather(own_sums, "bus", axis=0, tiled=True)
        real_cols = schur_inverse[0]
        imag_cols = schur_inverse[1]
        real_part = jnp.dot(real_cols, piece, precision=highest, preferred_element_type=jnp.float32)
        imag_part = jnp.dot(imag_cols, piece, precision=highest, preferred_element_type=jnp.float32)
        interface_own = real_part + rotate(imag_part)
        window = padded(interface_own, (("bus", 0),), if_rows)
        returned = jnp.dot(
            spread,
            admit(window[relative], adm_real, adm_imag),
            precision=highest,
            preferred_element_type=jnp.float32,
        )
        coeff = block_solve(block_inverse, driven + returned)
        coeffs.append(coeff)
        total = complex_mul(coeffs[1], inverses[degree - 1])
        for inner in range(2, degree + 1):
            total = total + complex_mul(coeffs[inner], inverses[degree - inner])
        inverses.append(-total)
    voltage = coeffs[0]
    for inner in range(1, ORDERS + 1):
        voltage = voltage + coeffs[inner]
    return (voltage[bus_slot], coeffs[-1][bus_slot])


def solution(mesh):
    in_specs = (
        P(("grp", "bus"), None),
        P(("grp", "bus")),
        P(("grp", "bus")),
        P(("grp", "bus"), None, None, None),
        P(None, ("grp", "bus"), None),
        P(("grp", "bus")),
        P(("grp", "bus")),
        P(None, ("grp", "bus")),
    )
    out_specs = (P(("grp", "bus"), None), P(("grp", "bus"), None))
    return jax.shard_map(local, mesh=mesh, in_specs=in_specs, out_specs=out_specs, check_vma=False)
```

profile of v0, /device:TPU:1, one launch (start us, length us, event | category | flops | bytes accessed | tf_op | source)
XLA Modules:
  0.0 191.1 jit_solution(1098834875355352029)
XLA Ops:
  0.7 0.7 copy-done.2
  1.4 3.8 %sort.17 = (s32[512]{0:T(512)}, s32[512]{0:T(512)S(1)}) sort(s32[512]{0:T(512)S(1)} %copy-done.2, s32[512]{0:T(512)S(1)} %iota.12), dimensions={0}, to_apply=%region_0.0 | sort | flops 4608 | bytes 8192 | tf_op jit(solution)/shard_map/jit(argsort)/sort | solution.py:77
  5.2 1.0 gather_fusion.1
  6.4 0.5 copy-done.11
  6.9 1.9 %gather_fusion.2 = s32[256]{0:T(256)S(1)} fusion(s32[512]{0:T(512)S(1)} %copy-done.2, s32[1024]{0:T(1024)S(1)} %pad_clamp_fusion.3), kind=kCustom, calls=%fused_computation.2 | custom fusion | bytes 3072 | tf_op jit(solution)/shard_map/gather | solution.py:80
  9.3 0.6 copy-done.1
  9.9 3.5 %gather_fusion = s32[512]{0:T(512)S(1)} fusion(s32[512]{0:T(512)S(1)} %copy-done.1, s32[1024]{0:T(1024)S(1)} %pad_clamp_fusion.4), kind=kCustom, calls=%fused_computation | custom fusion | bytes 6144 | tf_op jit(solution)/shard_map/gather | solution.py:79
  13.4 0.7 convolution_bitcast_fusion.14
  14.3 0.7 fusion.7
  14.9 0.7 gather_fusion.3
  15.8 0.7 copy-done.9
  16.5 0.7 copy-done.10
  17.6 2.1 %collective-permute-start.1 = (f32[64,128]{1,0:T(8,128)S(1)}, f32[64,128]{1,0:T(8,128)S(1)}, u32[]{:S(2)}, u32[]{:S(2)}) collective-permute-start(f32[64,128]{1,0:T(8,128)S(1)} %get-tuple-element.70), channel_id=1, source_target_pairs={{1,0},{2,1},{3,2},{4,3},{5,4},{6,5},{7,6},{8,7},{9,8},{10,9},{11,1... | collective-permute-start | bytes 98312 | tf_op jit(solution)/shard_map/ppermute | solution.py:15
  19.7 4.5 %collective-permute-start = (f32[64,128]{1,0:T(8,128)S(1)}, f32[64,128]{1,0:T(8,128)S(1)}, u32[]{:S(2)}, u32[]{:S(2)}) collective-permute-start(f32[64,128]{1,0:T(8,128)S(1)} %get-tuple-element.69), channel_id=1, source_target_pairs={{0,1},{1,2},{2,3},{3,4},{4,5},{5,6},{6,7},{7,8},{8,9},{9,10},{10,1... | collective-permute-start | bytes 98312 | tf_op jit(solution)/shard_map/ppermute | solution.py:15
  24.2 1.0 collective-permute-done
  25.2 24.1 %all_gather.12 = f32[1024,128]{1,0:T(8,128)S(1)} all-gather(f32[64,128]{1,0:T(8,128)S(1)} %fusion.148), channel_id=1, replica_groups=mesh['grp'=2,'bus'=16] {'bus'}, dimensions={0}, use_global_device_ids=true | all-gather | bytes 557056 | tf_op jit(solution)/shard_map/all_gather | solution.py:113
  50.3 2.1 %collective-permute-start.3 = (f32[64,128]{1,0:T(8,128)S(1)}, f32[64,128]{1,0:T(8,128)S(1)}, u32[]{:S(2)}, u32[]{:S(2)}) collective-permute-start(f32[64,128]{1,0:T(8,128)S(1)} %fusion.11), channel_id=1, source_target_pairs={{1,0},{2,1},{3,2},{4,3},{5,4},{6,5},{7,6},{8,7},{9,8},{10,9},{11,1... | collective-permute-start | bytes 98312 | tf_op jit(solution)/shard_map/ppermute | solution.py:26
  52.4 3.5 %collective-permute-start.2 = (f32[64,128]{1,0:T(8,128)S(1)}, f32[64,128]{1,0:T(8,128)S(1)}, u32[]{:S(2)}, u32[]{:S(2)}) collective-permute-start(f32[64,128]{1,0:T(8,128)S(1)} %fusion.11), channel_id=1, source_target_pairs={{0,1},{1,2},{2,3},{3,4},{4,5},{5,6},{6,7},{7,8},{8,9},{9,10},{10,1... | collective-permute-start | bytes 98312 | tf_op jit(solution)/shard_map/ppermute | solution.py:25
  55.9 1.0 collective-permute-done.2
  56.9 0.7 gather_fusion.4
  57.7 0.5 convolution_add_fusion.3
  59.9 0.7 convolution_bitcast_fusion.10
  60.7 0.7 fusion.5
  61.4 0.7 gather_fusion.5
  62.6 1.9 %collective-permute-start.5 = (f32[64,128]{1,0:T(8,128)S(1)}, f32[64,128]{1,0:T(8,128)S(1)}, u32[]{:S(2)}, u32[]{:S(2)}) collective-permute-start(f32[64,128]{1,0:T(8,128)S(1)} %get-tuple-element.68), channel_id=1, source_target_pairs={{1,0},{2,1},{3,2},{4,3},{5,4},{6,5},{7,6},{8,7},{9,8},{10,9},{11,1... | collective-permute-start | bytes 98312 | tf_op jit(solution)/shard_map/ppermute | solution.py:15
  64.6 4.2 %collective-permute-start.4 = (f32[64,128]{1,0:T(8,128)S(1)}, f32[64,128]{1,0:T(8,128)S(1)}, u32[]{:S(2)}, u32[]{:S(2)}) collective-permute-start(f32[64,128]{1,0:T(8,128)S(1)} %get-tuple-element.67), channel_id=1, source_target_pairs={{0,1},{1,2},{2,3},{3,4},{4,5},{5,6},{6,7},{7,8},{8,9},{9,10},{10,1... | collective-permute-start | bytes 98312 | tf_op jit(solution)/shard_map/ppermute | solution.py:15
  68.8 1.0 collective-permute-done.4
  69.8 21.1 %all_gather.13 = f32[1024,128]{1,0:T(8,128)S(1)} all-gather(f32[64,128]{1,0:T(8,128)S(1)} %fusion.147), channel_id=1, replica_groups=mesh['grp'=2,'bus'=16] {'bus'}, dimensions={0}, use_global_device_ids=true | all-gather | bytes 557056 | tf_op jit(solution)/shard_map/all_gather | solution.py:113
  91.4 0.5 fusion.10
  91.9 2.1 %collective-permute-start.7 = (f32[64,128]{1,0:T(8,128)S(1)}, f32[64,128]{1,0:T(8,128)S(1)}, u32[]{:S(2)}, u32[]{:S(2)}) collective-permute-start(f32[64,128]{1,0:T(8,128)S(1)} %fusion.10), channel_id=1, source_target_pairs={{1,0},{2,1},{3,2},{4,3},{5,4},{6,5},{7,6},{8,7},{9,8},{10,9},{11,1... | collective-permute-start | bytes 98312 | tf_op jit(solution)/shard_map/ppermute | solution.py:26
  94.0 3.7 %collective-permute-start.6 = (f32[64,128]{1,0:T(8,128)S(1)}, f32[64,128]{1,0:T(8,128)S(1)}, u32[]{:S(2)}, u32[]{:S(2)}) collective-permute-start(f32[64,128]{1,0:T(8,128)S(1)} %fusion.10), channel_id=1, source_target_pairs={{0,1},{1,2},{2,3},{3,4},{4,5},{5,6},{6,7},{7,8},{8,9},{9,10},{10,1... | collective-permute-start | bytes 98312 | tf_op jit(solution)/shard_map/ppermute | solution.py:25
  97.7 0.8 collective-permute-done.6
  98.5 0.7 gather_fusion.6
  99.3 0.5 convolution_add_fusion.2
  100.8 1.1 multiply_subtract_fusion.2
  102.2 1.0 multiply_subtract_fusion.4
  103.4 0.7 convolution_bitcast_fusion.6
  104.2 0.7 fusion.3
  104.9 0.7 gather_fusion.7
  106.2 1.9 %collective-permute-start.9 = (f32[64,128]{1,0:T(8,128)S(1)}, f32[64,128]{1,0:T(8,128)S(1)}, u32[]{:S(2)}, u32[]{:S(2)}) collective-permute-start(f32[64,128]{1,0:T(8,128)S(1)} %get-tuple-element.66), channel_id=1, source_target_pairs={{1,0},{2,1},{3,2},{4,3},{5,4},{6,5},{7,6},{8,7},{9,8},{10,9},{11,1... | collective-permute-start | bytes 98312 | tf_op jit(solution)/shard_map/ppermute | solution.py:15
  108.1 4.2 %collective-permute-start.8 = (f32[64,128]{1,0:T(8,128)S(1)}, f32[64,128]{1,0:T(8,128)S(1)}, u32[]{:S(2)}, u32[]{:S(2)}) collective-permute-start(f32[64,128]{1,0:T(8,128)S(1)} %get-tuple-element.65), channel_id=1, source_target_pairs={{0,1},{1,2},{2,3},{3,4},{4,5},{5,6},{6,7},{7,8},{8,9},{9,10},{10,1... | collective-permute-start | bytes 98312 | tf_op jit(solution)/shard_map/ppermute | solution.py:15
  112.3 1.0 collective-permute-done.8
  113.3 21.2 %all_gather.14 = f32[1024,128]{1,0:T(8,128)S(1)} all-gather(f32[64,128]{1,0:T(8,128)S(1)} %fusion.146), channel_id=1, replica_groups=mesh['grp'=2,'bus'=16] {'bus'}, dimensions={0}, use_global_device_ids=true | all-gather | bytes 557056 | tf_op jit(solution)/shard_map/all_gather | solution.py:113
  135.5 2.1 %collective-permute-start.11 = (f32[64,128]{1,0:T(8,128)S(1)}, f32[64,128]{1,0:T(8,128)S(1)}, u32[]{:S(2)}, u32[]{:S(2)}) collective-permute-start(f32[64,128]{1,0:T(8,128)S(1)} %fusion.9), channel_id=1, source_target_pairs={{1,0},{2,1},{3,2},{4,3},{5,4},{6,5},{7,6},{8,7},{9,8},{10,9},{11,1... | collective-permute-start | bytes 98312 | tf_op jit(solution)/shard_map/ppermute | solution.py:26
  137.6 3.5 %collective-permute-start.10 = (f32[64,128]{1,0:T(8,128)S(1)}, f32[64,128]{1,0:T(8,128)S(1)}, u32[]{:S(2)}, u32[]{:S(2)}) collective-permute-start(f32[64,128]{1,0:T(8,128)S(1)} %fusion.9), channel_id=1, source_target_pairs={{0,1},{1,2},{2,3},{3,4},{4,5},{5,6},{6,7},{7,8},{8,9},{9,10},{10,1... | collective-permute-start | bytes 98312 | tf_op jit(solution)/shard_map/ppermute | solution.py:25
  141.1 1.0 collective-permute-done.10
  142.1 0.7 gather_fusion.8
  142.9 0.5 convolution_add_fusion.1
  144.6 0.8 copy-done.5
  146.2 0.7 convolution_bitcast_fusion.2
  147.1 0.7 fusion.1
  147.7 0.7 gather_fusion.9
  149.0 1.9 %collective-permute-start.13 = (f32[64,128]{1,0:T(8,128)S(1)}, f32[64,128]{1,0:T(8,128)S(1)}, u32[]{:S(2)}, u32[]{:S(2)}) collective-permute-start(f32[64,128]{1,0:T(8,128)S(1)} %get-tuple-element.64), channel_id=1, source_target_pairs={{1,0},{2,1},{3,2},{4,3},{5,4},{6,5},{7,6},{8,7},{9,8},{10,9},{11,1... | collective-permute-start | bytes 98312 | tf_op jit(solution)/shard_map/ppermute | solution.py:15
  150.9 4.2 %collective-permute-start.12 = (f32[64,128]{1,0:T(8,128)S(1)}, f32[64,128]{1,0:T(8,128)S(1)}, u32[]{:S(2)}, u32[]{:S(2)}) collective-permute-start(f32[64,128]{1,0:T(8,128)S(1)} %get-tuple-element.63), channel_id=1, source_target_pairs={{0,1},{1,2},{2,3},{3,4},{4,5},{5,6},{6,7},{7,8},{8,9},{9,10},{10,1... | collective-permute-start | bytes 98312 | tf_op jit(solution)/shard_map/ppermute | solution.py:15
  155.2 1.0 collective-permute-done.12
  156.2 21.2 %all_gather.15 = f32[1024,128]{1,0:T(8,128)S(1)} all-gather(f32[64,128]{1,0:T(8,128)S(1)} %fusion.145), channel_id=1, replica_groups=mesh['grp'=2,'bus'=16] {'bus'}, dimensions={0}, use_global_device_ids=true | all-gather | bytes 557056 | tf_op jit(solution)/shard_map/all_gather | solution.py:113
  178.3 2.1 %collective-permute-start.15 = (f32[64,128]{1,0:T(8,128)S(1)}, f32[64,128]{1,0:T(8,128)S(1)}, u32[]{:S(2)}, u32[]{:S(2)}) collective-permute-start(f32[64,128]{1,0:T(8,128)S(1)} %fusion.8), channel_id=1, source_target_pairs={{1,0},{2,1},{3,2},{4,3},{5,4},{6,5},{7,6},{8,7},{9,8},{10,9},{11,1... | collective-permute-start | bytes 98312 | tf_op jit(solution)/shard_map/ppermute | solution.py:26
  180.4 3.5 %collective-permute-start.14 = (f32[64,128]{1,0:T(8,128)S(1)}, f32[64,128]{1,0:T(8,128)S(1)}, u32[]{:S(2)}, u32[]{:S(2)}) collective-permute-start(f32[64,128]{1,0:T(8,128)S(1)} %fusion.8), channel_id=1, source_target_pairs={{0,1},{1,2},{2,3},{3,4},{4,5},{5,6},{6,7},{7,8},{8,9},{9,10},{10,1... | collective-permute-start | bytes 98312 | tf_op jit(solution)/shard_map/ppermute | solution.py:25
  183.9 1.0 collective-permute-done.14
  184.9 0.7 gather_fusion.10
  185.7 0.5 convolution_add_fusion
  187.2 0.5 copy-done.8
  187.8 1.6 gather_fusion.11
  189.5 1.6 gather_fusion.12
  (109 shorter events, 13.1 us)
Async XLA Ops:
  0.6 4.5 %copy-start = (f32[512,128]{1,0:T(8,128)S(1)}, f32[512,128]{1,0:T(8,128)}, u32[]{:S(2)}) copy-start(f32[512,128]{1,0:T(8,128)} %param.8) | copy-start | bytes 786436
  0.6 0.7 copy-start.2
  6.2 0.7 copy-start.11
  9.2 0.7 copy-start.1
  9.9 3.5 %copy-start.3 = (f32[4,2,128,128]{3,2,1,0:T(8,128)S(1)}, f32[4,2,128,128]{3,2,1,0:T(8,128)}, u32[]{:S(2)}) copy-start(f32[4,2,128,128]{3,2,1,0:T(8,128)} %param.11) | copy-start | bytes 1572868
  15.8 0.7 copy-start.9
  16.5 0.7 copy-start.10
  17.5 31.8 %copy-start.4 = (f32[2,64,1024]{2,1,0:T(8,128)S(1)}, f32[2,64,1024]{2,1,0:T(8,128)}, u32[]{:S(2)}) copy-start(f32[2,64,1024]{2,1,0:T(8,128)} %param.12) | copy-start | bytes 1572868
  17.6 6.6 %collective-permute-start.1 = (f32[64,128]{1,0:T(8,128)S(1)}, f32[64,128]{1,0:T(8,128)S(1)}, u32[]{:S(2)}, u32[]{:S(2)}) collective-permute-start(f32[64,128]{1,0:T(8,128)S(1)} %get-tuple-element.70), channel_id=1, source_target_pairs={{1,0},{2,1},{3,2},{4,3},{5,4},{6,5},{7,6},{8,7},{9,8},{10,9},{11,1... | collective-permute-start | bytes 98312 | tf_op jit(solution)/shard_map/ppermute | solution.py:15
  19.7 5.5 %collective-permute-start = (f32[64,128]{1,0:T(8,128)S(1)}, f32[64,128]{1,0:T(8,128)S(1)}, u32[]{:S(2)}, u32[]{:S(2)}) collective-permute-start(f32[64,128]{1,0:T(8,128)S(1)} %get-tuple-element.69), channel_id=1, source_target_pairs={{0,1},{1,2},{2,3},{3,4},{4,5},{5,6},{6,7},{7,8},{8,9},{9,10},{10,1... | collective-permute-start | bytes 98312 | tf_op jit(solution)/shard_map/ppermute | solution.py:15
  50.3 5.6 %collective-permute-start.3 = (f32[64,128]{1,0:T(8,128)S(1)}, f32[64,128]{1,0:T(8,128)S(1)}, u32[]{:S(2)}, u32[]{:S(2)}) collective-permute-start(f32[64,128]{1,0:T(8,128)S(1)} %fusion.11), channel_id=1, source_target_pairs={{1,0},{2,1},{3,2},{4,3},{5,4},{6,5},{7,6},{8,7},{9,8},{10,9},{11,1... | collective-permute-start | bytes 98312 | tf_op jit(solution)/shard_map/ppermute | solution.py:26
  52.4 4.5 %collective-permute-start.2 = (f32[64,128]{1,0:T(8,128)S(1)}, f32[64,128]{1,0:T(8,128)S(1)}, u32[]{:S(2)}, u32[]{:S(2)}) collective-permute-start(f32[64,128]{1,0:T(8,128)S(1)} %fusion.11), channel_id=1, source_target_pairs={{0,1},{1,2},{2,3},{3,4},{4,5},{5,6},{6,7},{7,8},{8,9},{9,10},{10,1... | collective-permute-start | bytes 98312 | tf_op jit(solution)/shard_map/ppermute | solution.py:25
  62.6 6.2 %collective-permute-start.5 = (f32[64,128]{1,0:T(8,128)S(1)}, f32[64,128]{1,0:T(8,128)S(1)}, u32[]{:S(2)}, u32[]{:S(2)}) collective-permute-start(f32[64,128]{1,0:T(8,128)S(1)} %get-tuple-element.68), channel_id=1, source_target_pairs={{1,0},{2,1},{3,2},{4,3},{5,4},{6,5},{7,6},{8,7},{9,8},{10,9},{11,1... | collective-permute-start | bytes 98312 | tf_op jit(solution)/shard_map/ppermute | solution.py:15
  64.6 5.2 %collective-permute-start.4 = (f32[64,128]{1,0:T(8,128)S(1)}, f32[64,128]{1,0:T(8,128)S(1)}, u32[]{:S(2)}, u32[]{:S(2)}) collective-permute-start(f32[64,128]{1,0:T(8,128)S(1)} %get-tuple-element.67), channel_id=1, source_target_pairs={{0,1},{1,2},{2,3},{3,4},{4,5},{5,6},{6,7},{7,8},{8,9},{9,10},{10,1... | collective-permute-start | bytes 98312 | tf_op jit(solution)/shard_map/ppermute | solution.py:15
  91.9 5.8 %collective-permute-start.7 = (f32[64,128]{1,0:T(8,128)S(1)}, f32[64,128]{1,0:T(8,128)S(1)}, u32[]{:S(2)}, u32[]{:S(2)}) collective-permute-start(f32[64,128]{1,0:T(8,128)S(1)} %fusion.10), channel_id=1, source_target_pairs={{1,0},{2,1},{3,2},{4,3},{5,4},{6,5},{7,6},{8,7},{9,8},{10,9},{11,1... | collective-permute-start | bytes 98312 | tf_op jit(solution)/shard_map/ppermute | solution.py:26
  94.0 4.5 %collective-permute-start.6 = (f32[64,128]{1,0:T(8,128)S(1)}, f32[64,128]{1,0:T(8,128)S(1)}, u32[]{:S(2)}, u32[]{:S(2)}) collective-permute-start(f32[64,128]{1,0:T(8,128)S(1)} %fusion.10), channel_id=1, source_target_pairs={{0,1},{1,2},{2,3},{3,4},{4,5},{5,6},{6,7},{7,8},{8,9},{9,10},{10,1... | collective-permute-start | bytes 98312 | tf_op jit(solution)/shard_map/ppermute | solution.py:25
  106.2 6.2 %collective-permute-start.9 = (f32[64,128]{1,0:T(8,128)S(1)}, f32[64,128]{1,0:T(8,128)S(1)}, u32[]{:S(2)}, u32[]{:S(2)}) collective-permute-start(f32[64,128]{1,0:T(8,128)S(1)} %get-tuple-element.66), channel_id=1, source_target_pairs={{1,0},{2,1},{3,2},{4,3},{5,4},{6,5},{7,6},{8,7},{9,8},{10,9},{11,1... | collective-permute-start | bytes 98312 | tf_op jit(solution)/shard_map/ppermute | solution.py:15
  108.1 5.2 %collective-permute-start.8 = (f32[64,128]{1,0:T(8,128)S(1)}, f32[64,128]{1,0:T(8,128)S(1)}, u32[]{:S(2)}, u32[]{:S(2)}) collective-permute-start(f32[64,128]{1,0:T(8,128)S(1)} %get-tuple-element.65), channel_id=1, source_target_pairs={{0,1},{1,2},{2,3},{3,4},{4,5},{5,6},{6,7},{7,8},{8,9},{9,10},{10,1... | collective-permute-start | bytes 98312 | tf_op jit(solution)/shard_map/ppermute | solution.py:15
  135.5 5.6 %collective-permute-start.11 = (f32[64,128]{1,0:T(8,128)S(1)}, f32[64,128]{1,0:T(8,128)S(1)}, u32[]{:S(2)}, u32[]{:S(2)}) collective-permute-start(f32[64,128]{1,0:T(8,128)S(1)} %fusion.9), channel_id=1, source_target_pairs={{1,0},{2,1},{3,2},{4,3},{5,4},{6,5},{7,6},{8,7},{9,8},{10,9},{11,1... | collective-permute-start | bytes 98312 | tf_op jit(solution)/shard_map/ppermute | solution.py:26
  137.6 4.5 %collective-permute-start.10 = (f32[64,128]{1,0:T(8,128)S(1)}, f32[64,128]{1,0:T(8,128)S(1)}, u32[]{:S(2)}, u32[]{:S(2)}) collective-permute-start(f32[64,128]{1,0:T(8,128)S(1)} %fusion.9), channel_id=1, source_target_pairs={{0,1},{1,2},{2,3},{3,4},{4,5},{5,6},{6,7},{7,8},{8,9},{9,10},{10,1... | collective-permute-start | bytes 98312 | tf_op jit(solution)/shard_map/ppermute | solution.py:25
  144.4 1.0 copy-start.5
  144.4 1.0 copy-start.6
  144.4 1.1 copy-start.7
  149.0 6.2 %collective-permute-start.13 = (f32[64,128]{1,0:T(8,128)S(1)}, f32[64,128]{1,0:T(8,128)S(1)}, u32[]{:S(2)}, u32[]{:S(2)}) collective-permute-start(f32[64,128]{1,0:T(8,128)S(1)} %get-tuple-element.64), channel_id=1, source_target_pairs={{1,0},{2,1},{3,2},{4,3},{5,4},{6,5},{7,6},{8,7},{9,8},{10,9},{11,1... | collective-permute-start | bytes 98312 | tf_op jit(solution)/shard_map/ppermute | solution.py:15
  150.9 5.2 %collective-permute-start.12 = (f32[64,128]{1,0:T(8,128)S(1)}, f32[64,128]{1,0:T(8,128)S(1)}, u32[]{:S(2)}, u32[]{:S(2)}) collective-permute-start(f32[64,128]{1,0:T(8,128)S(1)} %get-tuple-element.63), channel_id=1, source_target_pairs={{0,1},{1,2},{2,3},{3,4},{4,5},{5,6},{6,7},{7,8},{8,9},{9,10},{10,1... | collective-permute-start | bytes 98312 | tf_op jit(solution)/shard_map/ppermute | solution.py:15
  178.3 5.6 %collective-permute-start.15 = (f32[64,128]{1,0:T(8,128)S(1)}, f32[64,128]{1,0:T(8,128)S(1)}, u32[]{:S(2)}, u32[]{:S(2)}) collective-permute-start(f32[64,128]{1,0:T(8,128)S(1)} %fusion.8), channel_id=1, source_target_pairs={{1,0},{2,1},{3,2},{4,3},{5,4},{6,5},{7,6},{8,7},{9,8},{10,9},{11,1... | collective-permute-start | bytes 98312 | tf_op jit(solution)/shard_map/ppermute | solution.py:26
  180.4 4.5 %collective-permute-start.14 = (f32[64,128]{1,0:T(8,128)S(1)}, f32[64,128]{1,0:T(8,128)S(1)}, u32[]{:S(2)}, u32[]{:S(2)}) collective-permute-start(f32[64,128]{1,0:T(8,128)S(1)} %fusion.8), channel_id=1, source_target_pairs={{0,1},{1,2},{2,3},{3,4},{4,5},{5,6},{6,7},{7,8},{8,9},{9,10},{10,1... | collective-permute-start | bytes 98312 | tf_op jit(solution)/shard_map/ppermute | solution.py:25
  186.8 1.0 copy-start.8
where the time goes:
time: 192 us; the launch traced here: 191 us
  blocking collectives  87.6 us (46%)
  starting transfers between devices  47.5 us (25%)
  local copies, waits for them, and re-layouts  21.4 us (11%)
  matrix products  15.8 us (8%)
  other arithmetic  9.73 us (5%)
  waiting for transfers between devices  7.73 us (4%)
    all_gather x4, blocking collectives, local(): piece = lax.all_gather(own_sums, 'bus', axis=0, tiled=True)  87.6 us
    ppermute x8, starting transfers between devices, shifted(): return lax.ppermute(block, axis, route)  25 us
    ppermute x4, starting transfers between devices, padded(): before = lax.ppermute(last, axis, up)  14.1 us
    ppermute x4, starting transfers between devices, padded(): after = lax.ppermute(initial, axis, down)  8.28 us
    unnamed x24, local copies, waits for them, and re-layouts  4.66 us
    dot_general x8, matrix products, block_solve(): jnp.einsum('pij,pjc->pic', inverse[:, 0], blocks, precision=highest, pref...  4.27 us
    dot_general x8, matrix products, block_solve(): jnp.einsum('pij,pjc->pic', inverse[:, 1], blocks, precision=highest, pref...  4.19 us
    ppermute x8, waiting for transfers between devices, shifted(): return lax.ppermute(block, axis, route)  3.97 us
  transfers between devices with their start and end apart: 16, of which 8 were waited for; matrix products, arithmetic and copies ran while one was open for 0% of the time, Pallas kernels for 0%

commit v1 on v0

v1 whole, which is shorter than its diff:
```python
import functools

import jax
import jax.numpy as jnp
from jax import lax
from jax.experimental import pallas as pl
from jax.experimental.pallas import tpu as pltpu
from jax.sharding import PartitionSpec as P

ORDERS = 4
INNER = 4
F32 = jnp.float32
BF16 = jnp.bfloat16
MESH = pl.DeviceIdType.MESH


def dot(a, b):
    return lax.dot_general(a, b, (((1,), (0,)), ((), ())), preferred_element_type=F32)


def dot_nt(a, b):
    return lax.dot_general(a, b, (((1,), (1,)), ((), ())), preferred_element_type=F32)


def split(x):
    high = x.astype(BF16)
    return high, (x - high.astype(F32)).astype(BF16)


def low_half(shape):
    return lax.broadcasted_iota(jnp.int32, shape, 1) < shape[1] // 2


def swap(x):
    return pltpu.roll(x, x.shape[1] // 2, 1)


def rotate(x):
    other = swap(x)
    return jnp.where(low_half(x.shape), -other, other)


def one_sided(select, x):
    high, low = split(x)
    out = dot(select, jnp.concatenate([high, low], axis=1))
    width = x.shape[1]
    return out[:, :width] + out[:, width:]


def dot3(a, b, mul):
    a_high, a_low = split(a)
    b_high, b_low = split(b)
    return mul(a_high, b_high) + (mul(a_high, b_low) + mul(a_low, b_high))


def complex_apply(high, low, x):
    width = x.shape[1]
    x_high, x_low = split(x)
    both = dot(high, jnp.concatenate([x_high, x_low], axis=1))
    out = both[:, :width] + (both[:, width:] + dot(low, x_high))
    rows = out.shape[0] // 2
    return out[:rows] + rotate(out[rows:])


def complex_mul(a, b):
    other = swap(a)
    low = low_half(a.shape)
    real = jnp.where(low, a, other)
    imag = jnp.where(low, -other, a)
    return real * b + imag * swap(b)


def kernel(
    n,
    loads, types, slots, block_inverse, schur, branch_bus, branch_iface, adm,
    voltage_out, last_out,
    perm, drv, mul_same, mul_swap, w_high, w_low, h_high, h_low, b_high, b_low,
    s_win, s_high, s_low, coeffs, terms, near, nb, gath,
    own_sem, s_send, s_recv, nb_send, nb_recv, z_send, z_recv, y_send, y_recv,
    c_send, c_recv, f_send, f_recv,
):
    outer_n = n // INNER
    me = lax.axis_index("bus")
    outer = me // INNER
    inner = me % INNER
    sib = me + 1 - 2 * (me % 2)
    pair = me + 2 - 4 * ((me // 2) % 2)
    pair_inner = pair % INNER
    bus_rows, columns = loads.shape
    if_rows = schur.shape[1]
    parts, pb = block_inverse.shape[0], block_inverse.shape[2]
    rows3 = 3 * if_rows
    pad = h_high.shape[1]

    def remote(src, dst, send, recv, device):
        return pltpu.make_async_remote_copy(
            src_ref=src, dst_ref=dst, send_sem=send, recv_sem=recv,
            device_id={"bus": device}, device_id_type=MESH,
        )

    def has_prev(fn):
        pl.when(me > 0)(fn)

    def has_next(fn):
        pl.when(me < n - 1)(fn)

    barrier = pltpu.get_barrier_semaphore()

    def greet(device):
        pl.semaphore_signal(barrier, inc=1, device_id={"bus": device}, device_id_type=MESH)

    has_prev(lambda: greet(me - 1))
    has_next(lambda: greet(me + 1))
    for j in range(1, outer_n):
        greet(((outer + j) % outer_n) * INNER + inner)
    greet(sib)
    greet(pair)
    own_copy = pltpu.make_async_copy(schur, s_win.at[1], own_sem)
    own_copy.start()
    edges = jnp.where(me > 0, 1, 0) + jnp.where(me < n - 1, 1, 0)
    pl.semaphore_wait(barrier, outer_n + 1 + edges)

    to_prev = remote(schur, s_win.at[2], s_send.at[0], s_recv.at[0], me - 1)
    to_next = remote(schur, s_win.at[0], s_send.at[1], s_recv.at[1], me + 1)
    has_prev(to_prev.start)
    has_next(to_next.start)

    slot = slots[...]
    kind = types[...]
    hit = lax.broadcasted_iota(jnp.int32, (bus_rows, bus_rows), 0) == slot
    ones = jnp.where(hit, 1.0, 0.0)
    perm[...] = ones.T.astype(BF16)
    place = ones.astype(BF16)
    load_place = jnp.where(kind == 0, ones, 0.0).astype(BF16)
    first_place = jnp.where(kind <= 1, ones, 0.0).astype(BF16)
    placed = one_sided(load_place, loads[...])
    first = one_sided(first_place, loads[...])
    low = low_half((bus_rows, columns))
    drv[...] = jnp.where(low, first, -first)
    other = swap(placed)
    mul_same[...] = jnp.where(low, -placed, other)
    mul_swap[...] = jnp.where(low, other, placed)

    branches = branch_bus.shape[1]
    at_bus = lax.broadcasted_iota(jnp.int32, (bus_rows, branches), 0) == branch_bus[...]
    spread = dot(place, jnp.where(at_bus, 1.0, 0.0).astype(BF16)).astype(BF16)
    relative = branch_iface[...] - (me - 1) * if_rows
    at_row = lax.broadcasted_iota(jnp.int32, (pad, branches), 0) == relative
    weights = jnp.concatenate(
        [jnp.where(at_row, adm[0:1, :], 0.0), jnp.where(at_row, adm[1:2, :], 0.0)], axis=0
    )
    weights_high, weights_low = split(weights)
    joins = dot_nt(weights_high, spread) + dot_nt(weights_low, spread)
    for p in range(parts):
        cols = slice(p * pb, (p + 1) * pb)
        inv_re, inv_im = block_inverse[p, 0], block_inverse[p, 1]
        high, lowp = split(jnp.concatenate([inv_re, inv_im], axis=0))
        b_high[p] = high
        b_low[p] = lowp
        g = joins[:, cols]
        q = dot3(g, jnp.concatenate([inv_re, inv_im], axis=1), dot)
        w_re = q[:rows3, :pb] - q[pad : pad + rows3, pb:]
        w_im = q[:rows3, pb:] + q[pad : pad + rows3, :pb]
        high, lowp = split(jnp.concatenate([w_re, w_im], axis=0))
        w_high[:, cols] = high
        w_low[:, cols] = lowp
        r = dot3(jnp.concatenate([inv_re, inv_im], axis=0), g, dot_nt)
        high, lowp = split(r[:pb, :pad] - r[pb:, pad:])
        h_high[p * pb : (p + 1) * pb, :] = high
        h_low[p * pb : (p + 1) * pb, :] = lowp
        high, lowp = split(r[:pb, pad:] + r[pb:, :pad])
        at = bus_rows + p * pb
        h_high[at : at + pb, :] = high
        h_low[at : at + pb, :] = lowp

    @pl.when(me == 0)
    def _():
        s_win[0] = jnp.zeros(s_win.shape[1:], F32)
        nb[:, 0] = jnp.zeros((ORDERS, if_rows, columns), F32)

    @pl.when(me == n - 1)
    def _():
        s_win[2] = jnp.zeros(s_win.shape[1:], F32)
        nb[:, 1] = jnp.zeros((ORDERS, if_rows, columns), F32)

    def order(t, carry):
        x = drv[...]
        near[t] = complex_apply(w_high[...], w_low[...], x)
        lower = remote(
            near.at[t, pl.ds(0, if_rows)], nb.at[t, 1], nb_send.at[t, 0], nb_recv.at[t, 0], me - 1
        )
        upper = remote(
            near.at[t, pl.ds(2 * if_rows, if_rows)],
            nb.at[t, 0], nb_send.at[t, 1], nb_recv.at[t, 1], me + 1,
        )
        has_prev(lower.start)
        has_next(upper.start)
        for p in range(parts):
            at = slice(p * pb, (p + 1) * pb)
            coeffs[t, at, :] = complex_apply(b_high[p], b_low[p], x[at])
        has_next(lower.wait_recv)
        has_prev(upper.wait_recv)
        gath[t, me] = near[t, if_rows : 2 * if_rows, :] + (nb[t, 0] + nb[t, 1])

        sends = []
        z_copies = []
        for j in range(1, outer_n):
            to = ((outer + j) % outer_n) * INNER + inner
            block = gath.at[t, me]
            copy = remote(block, block, z_send.at[t, j], z_recv.at[t, j], to)
            copy.start()
            z_copies.append(copy)
        y_copies = []
        for j in range(outer_n):
            if j:
                z_copies[j - 1].wait_recv()
            came = ((outer - j + outer_n) % outer_n) * INNER + inner
            block = gath.at[t, came]
            copy = remote(block, block, y_send.at[t, j], y_recv.at[t, j], pair)
            copy.start()
            y_copies.append(copy)
            copy = remote(block, block, c_send.at[t, j], c_recv.at[t, j], sib)
            copy.start()
            sends.append(copy)

        def earlier(k, total):
            return total + complex_mul(coeffs[k], terms[t - 1 - k])

        past = lax.fori_loop(0, t, earlier, jnp.zeros((bus_rows, columns), F32))
        terms[t] = -past

        @pl.when(t == 0)
        def _():
            own_copy.wait()
            has_next(to_prev.wait_recv)
            has_prev(to_next.wait_recv)
            for part in range(2):
                for w in range(3):
                    at = (part * 3 + w) * if_rows
                    high, lowp = split(s_win[w, part])
                    s_high[at : at + if_rows, :] = high
                    s_low[at : at + if_rows, :] = lowp

        f_copies = []
        for j in range(outer_n):
            y_copies[j].wait_recv()
            came = ((outer - j + outer_n) % outer_n) * INNER + pair_inner
            block = gath.at[t, came]
            copy = remote(block, block, f_send.at[t, j], f_recv.at[t, j], sib)
            copy.start()
            f_copies.append(copy)
        for copy in sends + f_copies:
            copy.wait_recv()

        sums = gath[t].reshape(n * if_rows, columns)
        window = complex_apply(s_high[...], s_low[...], sums)
        window = jnp.concatenate([window, jnp.zeros((pad - rows3, columns), F32)], axis=0)
        coeff = coeffs[t] + complex_apply(h_high[...], h_low[...], window)
        coeffs[t] = coeff
        term = coeff + terms[t]
        terms[t] = term
        drv[...] = mul_same[...] * term + mul_swap[...] * swap(term)

        has_prev(lower.wait_send)
        has_next(upper.wait_send)
        for copy in z_copies + y_copies + sends + f_copies:
            copy.wait_send()
        return carry

    lax.fori_loop(0, ORDERS, order, 0)

    has_prev(to_prev.wait_send)
    has_next(to_next.wait_send)
    total = jnp.where(low, 1.0, 0.0)
    for k in range(ORDERS):
        total = total + coeffs[k]
    voltage_out[...] = one_sided(perm[...], total)
    last_out[...] = one_sided(perm[...], coeffs[ORDERS - 1])


def local(
    loads, bus_type, bus_slot, block_inverse, schur_inverse, branch_bus, branch_iface, branch_adm
):
    n = lax.axis_size("bus")
    bus_rows, columns = loads.shape
    if_rows, iface = schur_inverse.shape[1:]
    parts, _, pb, _ = block_inverse.shape
    outer_n = n // INNER
    rows3 = 3 * if_rows
    pad = -(-rows3 // 128) * 128
    vmem = pl.BlockSpec(memory_space=pltpu.VMEM)
    dma = pltpu.SemaphoreType.DMA
    out = jax.ShapeDtypeStruct((bus_rows, columns), F32)
    return pl.pallas_call(
        functools.partial(kernel, n),
        out_shape=(out, out),
        in_specs=[vmem, vmem, vmem, vmem, pl.BlockSpec(memory_space=pl.ANY), vmem, vmem, vmem],
        out_specs=(vmem, vmem),
        scratch_shapes=[
            pltpu.VMEM((bus_rows, bus_rows), BF16),
            pltpu.VMEM((bus_rows, columns), F32),
            pltpu.VMEM((bus_rows, columns), F32),
            pltpu.VMEM((bus_rows, columns), F32),
            pltpu.VMEM((2 * rows3, bus_rows), BF16),
            pltpu.VMEM((2 * rows3, bus_rows), BF16),
            pltpu.VMEM((2 * bus_rows, pad), BF16),
            pltpu.VMEM((2 * bus_rows, pad), BF16),
            pltpu.VMEM((parts, 2 * pb, pb), BF16),
            pltpu.VMEM((parts, 2 * pb, pb), BF16),
            pltpu.VMEM((3, 2, if_rows, iface), F32),
            pltpu.VMEM((2 * rows3, iface), BF16),
            pltpu.VMEM((2 * rows3, iface), BF16),
            pltpu.VMEM((ORDERS, bus_rows, columns), F32),
            pltpu.VMEM((ORDERS, bus_rows, columns), F32),
            pltpu.VMEM((ORDERS, rows3, columns), F32),
            pltpu.VMEM((ORDERS, 2, if_rows, columns), F32),
            pltpu.VMEM((ORDERS, n, if_rows, columns), F32),
            dma, dma((2,)), dma((2,)),
            dma((ORDERS, 2)), dma((ORDERS, 2)),
            dma((ORDERS, outer_n)), dma((ORDERS, outer_n)),
            dma((ORDERS, outer_n)), dma((ORDERS, outer_n)),
            dma((ORDERS, outer_n)), dma((ORDERS, outer_n)),
            dma((ORDERS, outer_n)), dma((ORDERS, outer_n)),
        ],
        compiler_params=pltpu.CompilerParams(
            collective_id=0, has_side_effects=True, vmem_limit_bytes=48 * 1024 * 1024
        ),
        name="power_flow",
    )(
        loads,
        bus_type.reshape(1, bus_rows),
        bus_slot.reshape(1, bus_rows),
        block_inverse,
        schur_inverse,
        branch_bus.reshape(1, -1),
        branch_iface.reshape(1, -1),
        branch_adm,
    )


def solution(mesh):
    in_specs = (
        P(("grp", "bus"), None),
        P(("grp", "bus")),
        P(("grp", "bus")),
        P(("grp", "bus"), None, None, None),
        P(None, ("grp", "bus"), None),
        P(("grp", "bus")),
        P(("grp", "bus")),
        P(None, ("grp", "bus")),
    )
    out_specs = (P(("grp", "bus"), None), P(("grp", "bus"), None))
    return jax.shard_map(local, mesh=mesh, in_specs=in_specs, out_specs=out_specs, check_vma=False)
```

time: 192 us -> 74.9 us (0.39)
  blocking collectives: 87.6 us -> 0 us
  Pallas kernels: 0 us -> 68.1 us
  starting transfers between devices: 47.5 us -> 0 us
  matrix products: 15.8 us -> 0 us
  local copies, waits for them, and re-layouts: 21.4 us -> 5.81 us
  other arithmetic: 9.73 us -> 0 us
  waiting for transfers between devices: 7.73 us -> 0 us
    all_gather x4 -> x0, blocking collectives: 87.6 us -> none  [local(): piece = lax.all_gather(own_sums, 'bus', axis=0, tiled=True)]
    pallas_call x0 -> x1, Pallas kernels: none -> 68.1 us  [local(): pl.pallas_call(functools.partial(kernel, n), out_shape=(out, out), in_spe...]
    ppermute x16 -> x0, starting transfers between devices: 47.5 us -> none  [the longest x8 25 us: shifted(): return lax.ppermute(block, axis, route)]
    dot_general x32 -> x0, matrix products: 15.8 us -> none  [the longest x8 4.27 us: block_solve(): jnp.einsum('pij,pjc->pic', inverse[:, 0], blocks, precision=highest, pref...]
    gather x13 -> x0, local copies, waits for them, and re-layouts: 15.6 us -> none  [the longest x1 3.48 us: local(): placed_type = bus_type[placing]]
    ppermute x16 -> x0, waiting for transfers between devices: 7.73 us -> none  [the longest x8 3.97 us: shifted(): return lax.ppermute(block, axis, route)]
    sort x1 -> x0, other arithmetic: 3.77 us -> none  [local(): placing = jnp.argsort(bus_slot)]
    neg x23 -> x0, other arithmetic: 2.79 us -> none  [the longest x20 2.17 us: rotate(): return jnp.concatenate([-values[..., width:], values[..., :width]], axis=-1)]
  transfers between devices with their start and end apart: 16 -> 0, of which waited for: 8 -> 0; matrix products, arithmetic and copies ran while one was open for 0% -> 0% of each run, Pallas kernels for 0% -> 0%
where the time goes in v1:
time: 74.9 us; the launch traced here: 74.6 us
  Pallas kernels  68.1 us (91%)
  local copies, waits for them, and re-layouts  5.81 us (8%)
    pallas_call x1, Pallas kernels, local(): pl.pallas_call(functools.partial(kernel, n), out_shape=(out, out), in_spe...  68.1 us
    unnamed x18, local copies, waits for them, and re-layouts  5.81 us

profile of v1, /device:TPU:1, one launch (start us, length us, event | category | flops | bytes accessed | tf_op | source)
XLA Modules:
  0.0 74.6 jit_solution(12813851895688246400)
XLA Ops:
  0.6 0.0 copy-start.5
  0.6 0.0 copy-start.4
  0.7 0.0 copy-start.3
  0.7 0.0 copy-start.6
  0.7 0.6 copy-done.5
  1.3 0.0 copy-done.4
  1.3 0.0 copy-done.3
  1.3 0.0 copy-done.6
  1.4 0.0 copy-start
  1.4 1.0 %copy-done = f32[4,2,128,128]{3,2,1,0:T(8,128)S(1)} copy-done((f32[4,2,128,128]{3,2,1,0:T(8,128)S(1)}, f32[4,2,128,128]{3,2,1,0:T(8,128)}, u32[]{:S(2)}) %copy-start) | copy-done | bytes 524312
  2.4 0.0 copy-start.1
  2.4 1.0 %copy-done.1 = f32[2,64,1024]{2,1,0:T(8,128)S(1)} copy-done((f32[2,64,1024]{2,1,0:T(8,128)S(1)}, f32[2,64,1024]{2,1,0:T(8,128)}, u32[]{:S(2)}) %copy-start.1) | copy-done | bytes 524312
  3.4 0.0 copy-start.2
  3.4 0.9 %copy-done.2 = f32[512,128]{1,0:T(8,128)S(1)} copy-done((f32[512,128]{1,0:T(8,128)S(1)}, f32[512,128]{1,0:T(8,128)}, u32[]{:S(2)}) %copy-start.2) | copy-done | bytes 262168
  4.4 0.0 copy-start.7
  4.4 0.7 copy-done.7
  5.1 68.1 %power_flow.1 = (f32[512,128]{1,0:T(8,128)S(1)}, f32[512,128]{1,0:T(8,128)S(1)}) custom-call(f32[512,128]{1,0:T(8,128)S(1)} %copy-done.2, s32[1,512]{1,0:T(1,128)S(1)} %bitcast.4, s32[1,512]{1,0:T(1,128)S(1)} %bitcast.5, f32[4,2,128,128]{3,2,1,0:T(8,128)S(1)} %copy-done, f32[2,64,1024]{2,1,0:T(8,128)S(1)} %copy-done.1, s32[1,256]{1,0:T(1,128)S(1)} %bitcast.6, ...), custom_call_target="tpu_custom_call" | custom-call | tf_op jit(solution)/shard_map/power_flow/pallas_call | solution.py:294
  73.2 0.7 copy.12
  73.9 0.7 copy.13
Async XLA Ops:
  0.6 0.7 copy-start.5
  0.6 0.7 copy-start.4
  0.7 0.7 copy-start.3
  0.7 0.7 copy-start.6
  1.4 1.0 %copy-start = (f32[4,2,128,128]{3,2,1,0:T(8,128)S(1)}, f32[4,2,128,128]{3,2,1,0:T(8,128)}, u32[]{:S(2)}) copy-start(f32[4,2,128,128]{3,2,1,0:T(8,128)} %block_inverse.1) | copy-start | bytes 1572868
  2.4 1.0 %copy-start.1 = (f32[2,64,1024]{2,1,0:T(8,128)S(1)}, f32[2,64,1024]{2,1,0:T(8,128)}, u32[]{:S(2)}) copy-start(f32[2,64,1024]{2,1,0:T(8,128)} %schur.1) | copy-start | bytes 1572868
  3.4 0.9 %copy-start.2 = (f32[512,128]{1,0:T(8,128)S(1)}, f32[512,128]{1,0:T(8,128)}, u32[]{:S(2)}) copy-start(f32[512,128]{1,0:T(8,128)} %loads.1) | copy-start | bytes 786436
  4.4 0.7 copy-start.7

commit v2 on v1

--- a/solution.py
+++ b/solution.py
@@ -9,6 +9,7 @@
 
 ORDERS = 4
 INNER = 4
+CHUNKS = 16
 F32 = jnp.float32
 BF16 = jnp.bfloat16
 MESH = pl.DeviceIdType.MESH
@@ -72,8 +73,10 @@
 
 def kernel(
     n,
-    loads, types, slots, block_inverse, schur, branch_bus, branch_iface, adm,
+    loads_in, types_in, slots_in, inverse_in, schur, bus_in, iface_in, adm_in,
     voltage_out, last_out,
+    loads, types, slots, block_inverse, branch_bus, branch_iface, adm, in_sem,
+    joined, own_high, own_low, own_if, window_ref, i_send, i_recv,
     perm, drv, mul_same, mul_swap, w_high, w_low, h_high, h_low, b_high, b_low,
     s_win, s_high, s_low, coeffs, terms, near, nb, gath,
     own_sem, s_send, s_recv, nb_send, nb_recv, z_send, z_recv, y_send, y_recv,
@@ -104,6 +107,15 @@
     def has_next(fn):
         pl.when(me < n - 1)(fn)
 
+    arrays = (
+        (slots_in, slots), (types_in, types), (loads_in, loads), (bus_in, branch_bus),
+        (iface_in, branch_iface), (adm_in, adm), (inverse_in, block_inverse),
+    )
+    fetches = [
+        pltpu.make_async_copy(src, dst, in_sem.at[i]) for i, (src, dst) in enumerate(arrays)
+    ]
+    for fetch in fetches:
+        fetch.start()
     barrier = pltpu.get_barrier_semaphore()
 
     def greet(device):
@@ -120,11 +132,27 @@
     edges = jnp.where(me > 0, 1, 0) + jnp.where(me < n - 1, 1, 0)
     pl.semaphore_wait(barrier, outer_n + 1 + edges)
 
-    to_prev = remote(schur, s_win.at[2], s_send.at[0], s_recv.at[0], me - 1)
-    to_next = remote(schur, s_win.at[0], s_send.at[1], s_recv.at[1], me + 1)
-    has_prev(to_prev.start)
-    has_next(to_next.start)
-
+    to_prev, to_next = [], []
+    step = if_rows // (CHUNKS // 2)
+    for k in range(CHUNKS):
+        at = (k * 2 // CHUNKS, pl.ds(k % (CHUNKS // 2) * step, step))
+        src = schur.at[at]
+        to_prev.append(
+            remote(src, s_win.at[(2,) + at], s_send.at[0, k], s_recv.at[0, k], me - 1)
+        )
+        to_next.append(
+            remote(src, s_win.at[(0,) + at], s_send.at[1, k], s_recv.at[1, k], me + 1)
+        )
+
+    def start_chunks(first, last):
+        for k in range(first, last):
+            has_prev(to_prev[k].start)
+            has_next(to_next[k].start)
+
+    start_chunks(0, 8)
+
+    for fetch in fetches:
+        fetch.wait()
     slot = slots[...]
     kind = types[...]
     hit = lax.broadcasted_iota(jnp.int32, (bus_rows, bus_rows), 0) == slot
@@ -164,22 +192,20 @@
         high, lowp = split(jnp.concatenate([w_re, w_im], axis=0))
         w_high[:, cols] = high
         w_low[:, cols] = lowp
-        r = dot3(jnp.concatenate([inv_re, inv_im], axis=0), g, dot_nt)
-        high, lowp = split(r[:pb, :pad] - r[pb:, pad:])
-        h_high[p * pb : (p + 1) * pb, :] = high
-        h_low[p * pb : (p + 1) * pb, :] = lowp
-        high, lowp = split(r[:pb, pad:] + r[pb:, :pad])
-        at = bus_rows + p * pb
-        h_high[at : at + pb, :] = high
-        h_low[at : at + pb, :] = lowp
+
+    joined[...] = joins
+
+    window_ref[rows3:, :] = jnp.zeros((pad - rows3, columns), F32)
 
     @pl.when(me == 0)
     def _():
+        window_ref[:if_rows, :] = jnp.zeros((if_rows, columns), F32)
         s_win[0] = jnp.zeros(s_win.shape[1:], F32)
         nb[:, 0] = jnp.zeros((ORDERS, if_rows, columns), F32)
 
     @pl.when(me == n - 1)
     def _():
+        window_ref[2 * if_rows : rows3, :] = jnp.zeros((if_rows, columns), F32)
         s_win[2] = jnp.zeros(s_win.shape[1:], F32)
         nb[:, 1] = jnp.zeros((ORDERS, if_rows, columns), F32)
 
@@ -210,6 +236,7 @@
             copy = remote(block, block, z_send.at[t, j], z_recv.at[t, j], to)
             copy.start()
             z_copies.append(copy)
+        pl.when(t == 0)(lambda: start_chunks(8, 12))
         y_copies = []
         for j in range(outer_n):
             if j:
@@ -232,8 +259,28 @@
         @pl.when(t == 0)
         def _():
             own_copy.wait()
-            has_next(to_prev.wait_recv)
-            has_prev(to_next.wait_recv)
+            for part in range(2):
+                at = part * if_rows
+                high, lowp = split(s_win[1, part])
+                own_high[at : at + if_rows, :] = high
+                own_low[at : at + if_rows, :] = lowp
+            for p in range(parts):
+                inv_re, inv_im = block_inverse[p, 0], block_inverse[p, 1]
+                g = joined[:, p * pb : (p + 1) * pb]
+                r = dot3(jnp.concatenate([inv_re, inv_im], axis=0), g, dot_nt)
+                high, lowp = split(r[:pb, :pad] - r[pb:, pad:])
+                h_high[p * pb : (p + 1) * pb, :] = high
+                h_low[p * pb : (p + 1) * pb, :] = lowp
+                high, lowp = split(r[:pb, pad:] + r[pb:, :pad])
+                at = bus_rows + p * pb
+                h_high[at : at + pb, :] = high
+                h_low[at : at + pb, :] = lowp
+
+        @pl.when(t == 1)
+        def _():
+            for k in range(CHUNKS):
+                has_next(to_prev[k].wait_recv)
+                has_prev(to_next[k].wait_recv)
             for part in range(2):
                 for w in range(3):
                     at = (part * 3 + w) * if_rows
@@ -249,13 +296,33 @@
             copy = remote(block, block, f_send.at[t, j], f_recv.at[t, j], sib)
             copy.start()
             f_copies.append(copy)
+        pl.when(t == 0)(lambda: start_chunks(12, CHUNKS))
         for copy in sends + f_copies:
             copy.wait_recv()
 
         sums = gath[t].reshape(n * if_rows, columns)
-        window = complex_apply(s_high[...], s_low[...], sums)
-        window = jnp.concatenate([window, jnp.zeros((pad - rows3, columns), F32)], axis=0)
-        coeff = coeffs[t] + complex_apply(h_high[...], h_low[...], window)
+
+        @pl.when(t == 0)
+        def _():
+            own_if[...] = complex_apply(own_high[...], own_low[...], sums)
+            down = remote(
+                own_if, window_ref.at[pl.ds(2 * if_rows, if_rows)],
+                i_send.at[0], i_recv.at[0], me - 1,
+            )
+            up = remote(own_if, window_ref.at[pl.ds(0, if_rows)], i_send.at[1], i_recv.at[1], me + 1)
+            has_prev(down.start)
+            has_next(up.start)
+            window_ref[if_rows : 2 * if_rows, :] = own_if[...]
+            has_next(down.wait_recv)
+            has_prev(up.wait_recv)
+            has_prev(down.wait_send)
+            has_next(up.wait_send)
+
+        @pl.when(t > 0)
+        def _():
+            window_ref[:rows3, :] = complex_apply(s_high[...], s_low[...], sums)
+
+        coeff = coeffs[t] + complex_apply(h_high[...], h_low[...], window_ref[...])
         coeffs[t] = coeff
         term = coeff + terms[t]
         terms[t] = term
@@ -269,8 +336,9 @@
 
     lax.fori_loop(0, ORDERS, order, 0)
 
-    has_prev(to_prev.wait_send)
-    has_next(to_next.wait_send)
+    for k in range(CHUNKS):
+        has_prev(to_prev[k].wait_send)
+        has_next(to_next[k].wait_send)
     total = jnp.where(low, 1.0, 0.0)
     for k in range(ORDERS):
         total = total + coeffs[k]
@@ -285,8 +353,9 @@
     bus_rows, columns = loads.shape
     if_rows, iface = schur_inverse.shape[1:]
     parts, _, pb, _ = block_inverse.shape
+    branches = branch_bus.shape[0]
+    rows3 = 3 * if_rows
     outer_n = n // INNER
-    rows3 = 3 * if_rows
     pad = -(-rows3 // 128) * 128
     vmem = pl.BlockSpec(memory_space=pltpu.VMEM)
     dma = pltpu.SemaphoreType.DMA
@@ -294,9 +363,23 @@
     return pl.pallas_call(
         functools.partial(kernel, n),
         out_shape=(out, out),
-        in_specs=[vmem, vmem, vmem, vmem, pl.BlockSpec(memory_space=pl.ANY), vmem, vmem, vmem],
+        in_specs=[pl.BlockSpec(memory_space=pl.ANY)] * 8,
         out_specs=(vmem, vmem),
         scratch_shapes=[
+            pltpu.VMEM((bus_rows, columns), F32),
+            pltpu.VMEM((1, bus_rows), jnp.int32),
+            pltpu.VMEM((1, bus_rows), jnp.int32),
+            pltpu.VMEM(block_inverse.shape, F32),
+            pltpu.VMEM((1, branches), jnp.int32),
+            pltpu.VMEM((1, branches), jnp.int32),
+            pltpu.VMEM((2, branches), F32),
+            dma((7,)),
+            pltpu.VMEM((2 * pad, bus_rows), F32),
+            pltpu.VMEM((2 * if_rows, iface), BF16),
+            pltpu.VMEM((2 * if_rows, iface), BF16),
+            pltpu.VMEM((if_rows, columns), F32),
+            pltpu.VMEM((pad, columns), F32),
+            dma((2,)), dma((2,)),
             pltpu.VMEM((bus_rows, bus_rows), BF16),
             pltpu.VMEM((bus_rows, columns), F32),
             pltpu.VMEM((bus_rows, columns), F32),
@@ -315,7 +398,7 @@
             pltpu.VMEM((ORDERS, rows3, columns), F32),
             pltpu.VMEM((ORDERS, 2, if_rows, columns), F32),
             pltpu.VMEM((ORDERS, n, if_rows, columns), F32),
-            dma, dma((2,)), dma((2,)),
+            dma, dma((2, CHUNKS)), dma((2, CHUNKS)),
             dma((ORDERS, 2)), dma((ORDERS, 2)),
             dma((ORDERS, outer_n)), dma((ORDERS, outer_n)),
             dma((ORDERS, outer_n)), dma((ORDERS, outer_n)),
@@ -323,7 +406,7 @@
             dma((ORDERS, outer_n)), dma((ORDERS, outer_n)),
         ],
         compiler_params=pltpu.CompilerParams(
-            collective_id=0, has_side_effects=True, vmem_limit_bytes=48 * 1024 * 1024
+            collective_id=0, has_side_effects=True, vmem_limit_bytes=56 * 1024 * 1024
         ),
         name="power_flow",
     )(

time: 74.9 us -> 70.9 us (0.947)
  local copies, waits for them, and re-layouts: 5.81 us -> 2.42 us
    unnamed x18 -> x4, local copies, waits for them, and re-layouts: 5.81 us -> 2.42 us
where the time goes in v2:
time: 70.9 us; the launch traced here: 70.7 us
  Pallas kernels  67.7 us (95%)
  local copies, waits for them, and re-layouts  2.42 us (3%)
    pallas_call x1, Pallas kernels, local(): pl.pallas_call(functools.partial(kernel, n), out_shape=(out, out), in_spe...  67.7 us
    unnamed x4, local copies, waits for them, and re-layouts  2.42 us

profile of v2, /device:TPU:1, one launch (start us, length us, event | category | flops | bytes accessed | tf_op | source)
XLA Modules:
  0.0 70.7 jit_solution(15928864863016506974)
XLA Ops:
  0.6 67.7 %power_flow.1 = (f32[512,128]{1,0:T(8,128)}, f32[512,128]{1,0:T(8,128)}) custom-call(f32[512,128]{1,0:T(8,128)} %loads_in.1, s32[1,512]{1,0:T(1,128)} %bitcast.4, s32[1,512]{1,0:T(1,128)} %bitcast.5, f32[4,2,128,128]{3,2,1,0:T(8,128)} %inverse_in.1, f32[2,64,1024]{2,1,0:T(8,128)} %schur.1, s32[1,256]{1,0:T(1,128)} %bitcast.6, s32[1,256]{1,0:T(1,128)} %bitcast.7, ...), custom_call_target="tpu_custom_call" | custom-call | tf_op jit(solution)/shard_map/power_flow/pallas_call | solution.py:363
  68.3 0.0 copy-start
  68.3 1.7 %copy.12 = f32[512,128]{1,0:T(8,128)} copy(f32[512,128]{1,0:T(8,128)} %get-tuple-element.4) | data formatting | bytes 524288
  70.0 0.0 copy-done
  70.0 0.7 copy.13
Async XLA Ops:
  68.3 1.7 %copy-start = (f32[512,128]{1,0:T(8,128)S(1)}, f32[512,128]{1,0:T(8,128)}, u32[]{:S(2)}) copy-start(f32[512,128]{1,0:T(8,128)} %get-tuple-element.5) | copy-start | bytes 786436

commit v3 on v2

--- a/solution.py
+++ b/solution.py
@@ -157,7 +157,6 @@
     kind = types[...]
     hit = lax.broadcasted_iota(jnp.int32, (bus_rows, bus_rows), 0) == slot
     ones = jnp.where(hit, 1.0, 0.0)
-    perm[...] = ones.T.astype(BF16)
     place = ones.astype(BF16)
     load_place = jnp.where(kind == 0, ones, 0.0).astype(BF16)
     first_place = jnp.where(kind <= 1, ones, 0.0).astype(BF16)
@@ -182,14 +181,14 @@
     for p in range(parts):
         cols = slice(p * pb, (p + 1) * pb)
         inv_re, inv_im = block_inverse[p, 0], block_inverse[p, 1]
-        high, lowp = split(jnp.concatenate([inv_re, inv_im], axis=0))
-        b_high[p] = high
-        b_low[p] = lowp
         g = joins[:, cols]
         q = dot3(g, jnp.concatenate([inv_re, inv_im], axis=1), dot)
         w_re = q[:rows3, :pb] - q[pad : pad + rows3, pb:]
         w_im = q[:rows3, pb:] + q[pad : pad + rows3, :pb]
-        high, lowp = split(jnp.concatenate([w_re, w_im], axis=0))
+        mid = slice(if_rows, 2 * if_rows)
+        ends = (slice(0, if_rows), slice(2 * if_rows, rows3))
+        w = [w_re[at] for at in ends] + [w_im[at] for at in ends] + [w_re[mid], w_im[mid]]
+        high, lowp = split(jnp.concatenate(w, axis=0))
         w_high[:, cols] = high
         w_low[:, cols] = lowp
 
@@ -211,26 +210,36 @@
 
     def order(t, carry):
         x = drv[...]
-        near[t] = complex_apply(w_high[...], w_low[...], x)
+        cut = 4 * if_rows
+        near[t, : 2 * if_rows, :] = complex_apply(w_high[:cut, :], w_low[:cut, :], x)
         lower = remote(
             near.at[t, pl.ds(0, if_rows)], nb.at[t, 1], nb_send.at[t, 0], nb_recv.at[t, 0], me - 1
         )
         upper = remote(
-            near.at[t, pl.ds(2 * if_rows, if_rows)],
+            near.at[t, pl.ds(if_rows, if_rows)],
             nb.at[t, 0], nb_send.at[t, 1], nb_recv.at[t, 1], me + 1,
         )
         has_prev(lower.start)
         has_next(upper.start)
+        near[t, 2 * if_rows :, :] = complex_apply(w_high[cut:, :], w_low[cut:, :], x)
+
+        @pl.when(t == 0)
+        def _():
+            for p in range(parts):
+                stacked = block_inverse[p].reshape(2 * pb, pb)
+                b_high[p], b_low[p] = split(stacked)
+
         for p in range(parts):
             at = slice(p * pb, (p + 1) * pb)
             coeffs[t, at, :] = complex_apply(b_high[p], b_low[p], x[at])
         has_next(lower.wait_recv)
         has_prev(upper.wait_recv)
-        gath[t, me] = near[t, if_rows : 2 * if_rows, :] + (nb[t, 0] + nb[t, 1])
+        gath[t, me] = near[t, 2 * if_rows :, :] + (nb[t, 0] + nb[t, 1])
 
         sends = []
         z_copies = []
-        for j in range(1, outer_n):
+        steps = sorted(range(1, outer_n), key=lambda j: (min(j, outer_n - j), j))
+        for j in steps:
             to = ((outer + j) % outer_n) * INNER + inner
             block = gath.at[t, me]
             copy = remote(block, block, z_send.at[t, j], z_recv.at[t, j], to)
@@ -238,9 +247,9 @@
             z_copies.append(copy)
         pl.when(t == 0)(lambda: start_chunks(8, 12))
         y_copies = []
-        for j in range(outer_n):
-            if j:
-                z_copies[j - 1].wait_recv()
+        for i, j in enumerate([0] + steps):
+            if i:
+                z_copies[i - 1].wait_recv()
             came = ((outer - j + outer_n) % outer_n) * INNER + inner
             block = gath.at[t, came]
             copy = remote(block, block, y_send.at[t, j], y_recv.at[t, j], pair)
@@ -259,6 +268,8 @@
         @pl.when(t == 0)
         def _():
             own_copy.wait()
+            rows = lax.broadcasted_iota(jnp.int32, (bus_rows, bus_rows), 0)
+            perm[...] = jnp.where(rows == slots[...], 1.0, 0.0).T.astype(BF16)
             for part in range(2):
                 at = part * if_rows
                 high, lowp = split(s_win[1, part])
@@ -289,22 +300,33 @@
                     s_low[at : at + if_rows, :] = lowp
 
         f_copies = []
-        for j in range(outer_n):
-            y_copies[j].wait_recv()
+        for i, j in enumerate([0] + steps):
+            y_copies[i].wait_recv()
             came = ((outer - j + outer_n) % outer_n) * INNER + pair_inner
             block = gath.at[t, came]
             copy = remote(block, block, f_send.at[t, j], f_recv.at[t, j], sib)
             copy.start()
             f_copies.append(copy)
         pl.when(t == 0)(lambda: start_chunks(12, CHUNKS))
-        for copy in sends + f_copies:
-            copy.wait_recv()
-
-        sums = gath[t].reshape(n * if_rows, columns)
+        group = INNER * if_rows
+
+        def arrived(i):
+            j = ([0] + steps)[i]
+            sends[i].wait_recv()
+            f_copies[i].wait_recv()
+            came = (outer - j + outer_n) % outer_n
+            cols = pl.ds(pl.multiple_of(came * group, group), group)
+            return cols, gath[t, pl.ds(came * INNER, INNER)].reshape(group, columns)
+
 
         @pl.when(t == 0)
         def _():
-            own_if[...] = complex_apply(own_high[...], own_low[...], sums)
+            total = None
+            for j in range(outer_n):
+                cols, sums = arrived(j)
+                part = complex_apply(own_high[:, cols], own_low[:, cols], sums)
+                total = part if total is None else total + part
+            own_if[...] = total
             down = remote(
                 own_if, window_ref.at[pl.ds(2 * if_rows, if_rows)],
                 i_send.at[0], i_recv.at[0], me - 1,
@@ -320,7 +342,12 @@
 
         @pl.when(t > 0)
         def _():
-            window_ref[:rows3, :] = complex_apply(s_high[...], s_low[...], sums)
+            total = None
+            for j in range(outer_n):
+                cols, sums = arrived(j)
+                part = complex_apply(s_high[:, cols], s_low[:, cols], sums)
+                total = part if total is None else total + part
+            window_ref[:rows3, :] = total
 
         coeff = coeffs[t] + complex_apply(h_high[...], h_low[...], window_ref[...])
         coeffs[t] = coeff

time: 70.9 us -> 69.6 us (0.982)
  Pallas kernels: 67.7 us -> 66.2 us
    pallas_call x1, Pallas kernels: 67.7 us -> 66.2 us  [local(): pl.pallas_call(functools.partial(kernel, n), out_shape=(out, out), in_spe...]
where the time goes in v3:
time: 69.6 us; the launch traced here: 69.2 us
  Pallas kernels  66.2 us (95%)
  local copies, waits for them, and re-layouts  2.42 us (3%)
    pallas_call x1, Pallas kernels, local(): pl.pallas_call(functools.partial(kernel, n), out_shape=(out, out), in_spe...  66.2 us
    unnamed x4, local copies, waits for them, and re-layouts  2.42 us

profile of v3, /device:TPU:1, one launch (start us, length us, event | category | flops | bytes accessed | tf_op | source)
XLA Modules:
  0.0 69.2 jit_solution(11892845057554817834)
XLA Ops:
  0.6 66.2 %power_flow.1 = (f32[512,128]{1,0:T(8,128)}, f32[512,128]{1,0:T(8,128)}) custom-call(f32[512,128]{1,0:T(8,128)} %loads_in.1, s32[1,512]{1,0:T(1,128)} %bitcast.4, s32[1,512]{1,0:T(1,128)} %bitcast.5, f32[4,2,128,128]{3,2,1,0:T(8,128)} %inverse_in.1, f32[2,64,1024]{2,1,0:T(8,128)} %schur.1, s32[1,256]{1,0:T(1,128)} %bitcast.6, s32[1,256]{1,0:T(1,128)} %bitcast.7, ...), custom_call_target="tpu_custom_call" | custom-call | tf_op jit(solution)/shard_map/power_flow/pallas_call | solution.py:390
  66.8 0.0 copy-start
  66.8 1.7 %copy.12 = f32[512,128]{1,0:T(8,128)} copy(f32[512,128]{1,0:T(8,128)} %get-tuple-element.4) | data formatting | bytes 524288
  68.5 0.0 copy-done
  68.5 0.7 %copy.13 = f32[512,128]{1,0:T(8,128)} copy(f32[512,128]{1,0:T(8,128)S(1)} %copy-done) | data formatting | bytes 524288
Async XLA Ops:
  66.8 1.7 %copy-start = (f32[512,128]{1,0:T(8,128)S(1)}, f32[512,128]{1,0:T(8,128)}, u32[]{:S(2)}) copy-start(f32[512,128]{1,0:T(8,128)} %get-tuple-element.5) | copy-start | bytes 786436

commit v4 on v3

--- a/solution.py
+++ b/solution.py
@@ -287,6 +287,13 @@
                 h_high[at : at + pb, :] = high
                 h_low[at : at + pb, :] = lowp
 
+        @pl.when(t == ORDERS - 1)
+        def _():
+            total = jnp.where(low_half((bus_rows, columns)), 1.0, 0.0)
+            for k in range(ORDERS - 1):
+                total = total + coeffs[k]
+            voltage_out[...] = one_sided(perm[...], total)
+
         @pl.when(t == 1)
         def _():
             for k in range(CHUNKS):
@@ -351,9 +358,12 @@
 
         coeff = coeffs[t] + complex_apply(h_high[...], h_low[...], window_ref[...])
         coeffs[t] = coeff
-        term = coeff + terms[t]
-        terms[t] = term
-        drv[...] = mul_same[...] * term + mul_swap[...] * swap(term)
+
+        @pl.when(t < ORDERS - 1)
+        def _():
+            term = coeffs[t] + terms[t]
+            terms[t] = term
+            drv[...] = mul_same[...] * term + mul_swap[...] * swap(term)
 
         has_prev(lower.wait_send)
         has_next(upper.wait_send)
@@ -366,11 +376,9 @@
     for k in range(CHUNKS):
         has_prev(to_prev[k].wait_send)
         has_next(to_next[k].wait_send)
-    total = jnp.where(low, 1.0, 0.0)
-    for k in range(ORDERS):
-        total = total + coeffs[k]
-    voltage_out[...] = one_sided(perm[...], total)
-    last_out[...] = one_sided(perm[...], coeffs[ORDERS - 1])
+    last = one_sided(perm[...], coeffs[ORDERS - 1])
+    last_out[...] = last
+    voltage_out[...] += last
 
 
 def local(

time: 69.6 us -> 69.6 us (level)
  no operation moved by 1% of the time
where the time goes in v4:
time: 69.6 us; the launch traced here: 69.2 us
  Pallas kernels  66.1 us (95%)
  local copies, waits for them, and re-layouts  2.42 us (3%)
    pallas_call x1, Pallas kernels, local(): pl.pallas_call(functools.partial(kernel, n), out_shape=(out, out), in_spe...  66.1 us
    unnamed x4, local copies, waits for them, and re-layouts  2.42 us

profile of v4, /device:TPU:1, one launch (start us, length us, event | category | flops | bytes accessed | tf_op | source)
XLA Modules:
  0.0 69.2 jit_solution(17703557159364050279)
XLA Ops:
  0.6 66.1 %power_flow.1 = (f32[512,128]{1,0:T(8,128)}, f32[512,128]{1,0:T(8,128)}) custom-call(f32[512,128]{1,0:T(8,128)} %loads_in.1, s32[1,512]{1,0:T(1,128)} %bitcast.4, s32[1,512]{1,0:T(1,128)} %bitcast.5, f32[4,2,128,128]{3,2,1,0:T(8,128)} %inverse_in.1, f32[2,64,1024]{2,1,0:T(8,128)} %schur.1, s32[1,256]{1,0:T(1,128)} %bitcast.6, s32[1,256]{1,0:T(1,128)} %bitcast.7, ...), custom_call_target="tpu_custom_call" | custom-call | tf_op jit(solution)/shard_map/power_flow/pallas_call | solution.py:398
  66.8 0.0 copy-start
  66.8 1.7 %copy.12 = f32[512,128]{1,0:T(8,128)} copy(f32[512,128]{1,0:T(8,128)} %get-tuple-element.4) | data formatting | bytes 524288
  68.5 0.0 copy-done
  68.5 0.7 %copy.13 = f32[512,128]{1,0:T(8,128)} copy(f32[512,128]{1,0:T(8,128)S(1)} %copy-done) | data formatting | bytes 524288
Async XLA Ops:
  66.8 1.7 %copy-start = (f32[512,128]{1,0:T(8,128)S(1)}, f32[512,128]{1,0:T(8,128)}, u32[]{:S(2)}) copy-start(f32[512,128]{1,0:T(8,128)} %get-tuple-element.5) | copy-start | bytes 786436
